TPU v7x, 32 devices: a whole 2x2x4 slice. The times are simulated.
32 devices in a mesh: row: 8 (over z, x), col: 4 (over y, core).
Axes of the slice: x: 2, y: 2, z: 4, core: 2. Of those that a mesh axis runs over, the one named last changes fastest.
Arguments:
- tiles: bfloat16 [8, 4, 64, 128, 128], P('row', 'col'), may hold values from -0.078125 to 0.078125
- positions: int32 [8, 4, 64], replicated, may hold values from 0 to 15, as said below
- demand: bfloat16 [16384, 128], P(('row', 'col')), may hold values from -6 to 6
- value_added: bfloat16 [16384, 128], P(('row', 'col')), may hold values from -6 to 6
- extracted: int32 [128], replicated, may hold values from 0 to 127
Outputs:
- quantity: float32 [16384, 128], P(('row', 'col'))
- price: float32 [16384, 128], P(('row', 'col'))
Inputs may be any that keep to these rules, and one draw needn't show every extreme that they name: Within each device's slots d * 2 to d * 2 + 1 the 2 positions differ.
All inputs are finite; a program needn't handle non-finite values.
Results may differ from a plain program's by a relative error of at most 0.0011.
Values may be sent and summed in bfloat16 or wider, within the bound.
A program may use at most 192 MiB of HBM per device.

v0:
```python
import jax
import jax.numpy as jnp
from jax import lax
from jax.sharding import PartitionSpec as P

TERMS = 3
GROUPS = 128


def supply_term(vector, own_tiles, local_rows, local_columns, block_rows, tile_size):
    scenarios = vector.shape[1]
    gathered = lax.all_gather(vector, "row", axis=0, tiled=True)
    picked = gathered.reshape(-1, tile_size, scenarios)[local_columns]
    products = jnp.einsum("ntk,nks->nts", own_tiles, picked, preferred_element_type=jnp.float32)
    selector = (jnp.arange(block_rows, dtype=jnp.int32)[:, None] == local_rows[None, :]).astype(
        jnp.float32
    )
    partial_value = jnp.einsum("rn,nts->rts", selector, products, precision=lax.Precision.HIGHEST)
    return lax.psum_scatter(
        partial_value.reshape(-1, scenarios), "col", scatter_dimension=0, tiled=True
    )


def charge_term(vector, moved_tiles, local_rows, local_columns, block_rows, tile_size):
    scenarios = vector.shape[1]
    gathered = lax.all_gather(vector, "row", axis=0, tiled=True)
    picked = gathered.reshape(-1, tile_size, scenarios)[local_columns]
    products = jnp.einsum("nkt,nks->nts", moved_tiles, picked, preferred_element_type=jnp.float32)
    selector = (jnp.arange(block_rows, dtype=jnp.int32)[:, None] == local_rows[None, :]).astype(
        jnp.float32
    )
    partial_value = jnp.einsum("rn,nts->rts", selector, products, precision=lax.Precision.HIGHEST)
    return lax.psum_scatter(
        partial_value.reshape(-1, scenarios), "col", scatter_dimension=0, tiled=True
    )


def shards(tiles, positions, demand, value_added, extracted):
    row_devices = lax.axis_size("row")
    column_devices = lax.axis_size("col")
    row_index = lax.axis_index("row")
    column_index = lax.axis_index("col")
    tile_size = tiles.shape[-1]
    slot_count = tiles.shape[2]
    own_tiles = tiles.reshape(slot_count, tile_size, tile_size)
    scenarios = demand.shape[1]
    quarter = demand.shape[0] // tile_size
    block_rows = quarter * column_devices
    capacity = slot_count // (row_devices * column_devices)
    slot_index = jnp.arange(slot_count, dtype=jnp.int32)
    target = slot_index // capacity
    own_places = lax.dynamic_slice(
        positions, (row_index, column_index, 0), (1, 1, slot_count)
    ).reshape(slot_count)
    local_rows = target % column_devices * quarter + own_places // quarter
    local_columns = target // column_devices * quarter + own_places % quarter
    first_block = row_index * block_rows + column_index * quarter
    blocks = first_block + jnp.arange(quarter, dtype=jnp.int32)
    keep_mask = (blocks[:, None] % GROUPS != extracted[None, :]).astype(jnp.float32)[:, None, :]
    quantity = (
        keep_mask * demand.reshape(quarter, tile_size, scenarios).astype(jnp.float32)
    ).reshape(-1, scenarios)
    move = quantity.astype(jnp.bfloat16)
    for term_number in range(TERMS):
        image = supply_term(move, own_tiles, local_rows, local_columns, block_rows, tile_size)
        masked = (keep_mask * image.reshape(quarter, tile_size, scenarios)).reshape(-1, scenarios)
        quantity = quantity + masked
        if term_number + 1 < TERMS:
            move = masked.astype(jnp.bfloat16)
    price = (
        keep_mask * value_added.reshape(quarter, tile_size, scenarios).astype(jnp.float32)
    ).reshape(-1, scenarios)
    charge = price.astype(jnp.bfloat16)
    moved_tiles = lax.all_to_all(own_tiles, ("row", "col"), split_axis=0, concat_axis=0, tiled=True)
    self_index = row_index * column_devices + column_index
    table = positions.reshape(row_devices * column_devices, slot_count)
    arrived = lax.dynamic_slice_in_dim(table, self_index * capacity, capacity, axis=1).reshape(
        slot_count
    )
    source_row = target // column_devices
    source_column = target % column_devices
    moved_rows = source_column * quarter + arrived % quarter
    moved_columns = source_row * quarter + arrived // quarter
    for term_number in range(TERMS):
        cost_image = charge_term(
            charge, moved_tiles, moved_rows, moved_columns, block_rows, tile_size
        )
        masked = (keep_mask * cost_image.reshape(quarter, tile_size, scenarios)).reshape(
            -1, scenarios
        )
        price = price + masked
        if term_number + 1 < TERMS:
            charge = masked.astype(jnp.bfloat16)
    return (quantity, price)


def solution(mesh):
    placed = (
        P("row", "col", None, None, None),
        P(),
        P(("row", "col"), None),
        P(("row", "col"), None),
        P(),
    )
    return jax.shard_map(
        shards,
        mesh=mesh,
        in_specs=placed,
        out_specs=(P(("row", "col"), None), P(("row", "col"), None)),
        check_vma=False,
    )
```

profile of v0, /device:TPU:1, one launch (start us, length us, event | category | flops | bytes accessed | tf_op | source)
XLA Modules:
  0.0 447.9 jit_solution(699449108784459341)
XLA Ops:
  9.7 7.2 %all-to-all-start = ((bf16[64,128,128]{2,1,0:T(8,128)(2,1)}), bf16[64,128,128]{2,1,0:T(8,128)(2,1)}, u32[]{:S(2)}, u32[]{:S(2)}) async-start(bf16[64,128,128]{2,1,0:T(8,128)(2,1)} %bitcast.112), calls=%async_computation.3 | async-start | bytes 4194304 | tf_op jit(solution)/shard_map/all_to_all | solution.py:74
  17.8 51.3 %all-gather.7.cloned.1.call-done = bf16[4096,128]{1,0:T(8,128)(2,1)} async-done(((bf16[512,128]{1,0:T(8,128)(2,1)}), bf16[4096,128]{1,0:T(8,128)(2,1)}) %all-gather.7.cloned.1.call-update) | async-done | bytes 1048592 | tf_op jit(solution)/shard_map/all_gather | solution.py:12
  69.0 3.6 gather_fusion
  72.6 5.1 %fusion.49 = f32[64,128,128]{2,1,0:T(8,128)} fusion(bf16[64,128,128]{2,1,0:T(8,128)(2,1)} %gather_fusion, bf16[1,1,64,128,128]{4,3,2,1,0:T(8,128)(2,1)S(1)} %copy-done), kind=kOutput, calls=%fused_computation.99 | convolution fusion | flops 268435456 | bytes 8388608 | tf_op jit(solution)/shard_map/ntk,nks->nts/dot_general | solution.py:14
  77.8 5.4 %copy.13 = f32[64,128,128]{1,0,2:T(8,128)} copy(f32[64,128,128]{2,1,0:T(8,128)} %fusion.49) | data formatting | bytes 8388608 | tf_op jit(solution)/shard_map/ntk,nks->nts/dot_general | solution.py:14
  83.1 3.7 fusion.10
  88.5 19.8 %all-gather.13.cloned.1.call-done = bf16[4096,128]{1,0:T(8,128)(2,1)} async-done(((bf16[512,128]{1,0:T(8,128)(2,1)}), bf16[4096,128]{1,0:T(8,128)(2,1)}) %all-gather.13.cloned.1.call-update) | async-done | bytes 1048592 | tf_op jit(solution)/shard_map/all_gather | solution.py:26
  111.7 5.1 %fusion.51 = f32[64,128,128]{2,1,0:T(8,128)} fusion(bf16[64,128,128]{2,1,0:T(8,128)(2,1)} %gather_fusion.3, bf16[64,128,128]{2,1,0:T(8,128)(2,1)} %all-to-all-done), kind=kOutput, calls=%fused_computation.101 | convolution fusion | flops 268435456 | bytes 8388608 | tf_op jit(solution)/shard_map/nkt,nks->nts/dot_general | solution.py:28
  116.8 5.5 %copy.16 = f32[64,128,128]{1,0,2:T(8,128)} copy(f32[64,128,128]{2,1,0:T(8,128)} %fusion.51) | data formatting | bytes 8388608 | tf_op jit(solution)/shard_map/nkt,nks->nts/dot_general | solution.py:28
  122.3 3.7 fusion.4
  127.3 8.2 %reduce-scatter.7.cloned.1.call-done = f32[512,128]{1,0:T(8,128)} async-done(((f32[2048,128]{1,0:T(8,128)}), f32[512,128]{1,0:T(8,128)}) %reduce-scatter.7.cloned.1.call-update) | async-done | bytes 262160 | tf_op jit(solution)/shard_map/reduce_scatter | solution.py:19
  135.5 27.5 %reduce-scatter.13.cloned.1.call-done = f32[512,128]{1,0:T(8,128)} async-done(((f32[2048,128]{1,0:T(8,128)}), f32[512,128]{1,0:T(8,128)}) %reduce-scatter.13.cloned.1.call-update) | async-done | bytes 262160 | tf_op jit(solution)/shard_map/reduce_scatter | solution.py:33
  165.6 39.1 %all-gather.15.cloned.1.call-done = bf16[4096,128]{1,0:T(8,128)(2,1)} async-done(((bf16[512,128]{1,0:T(8,128)(2,1)}), bf16[4096,128]{1,0:T(8,128)(2,1)}) %all-gather.15.cloned.1.call-update) | async-done | bytes 1048592 | tf_op jit(solution)/shard_map/all_gather | solution.py:26
  208.1 5.1 %fusion.52 = f32[64,128,128]{2,1,0:T(8,128)} fusion(bf16[64,128,128]{2,1,0:T(8,128)(2,1)} %gather_fusion.4, bf16[64,128,128]{2,1,0:T(8,128)(2,1)} %all-to-all-done), kind=kOutput, calls=%fused_computation.102 | convolution fusion | flops 268435456 | bytes 8388608 | tf_op jit(solution)/shard_map/nkt,nks->nts/dot_general | solution.py:28
  213.2 5.4 %copy.17 = f32[64,128,128]{1,0,2:T(8,128)} copy(f32[64,128,128]{2,1,0:T(8,128)} %fusion.52) | data formatting | bytes 8388608 | tf_op jit(solution)/shard_map/nkt,nks->nts/dot_general | solution.py:28
  218.6 3.7 fusion.2
  223.7 22.5 %all-gather.9.cloned.1.call-done = bf16[4096,128]{1,0:T(8,128)(2,1)} async-done(((bf16[512,128]{1,0:T(8,128)(2,1)}), bf16[4096,128]{1,0:T(8,128)(2,1)}) %all-gather.9.cloned.1.call-update) | async-done | bytes 1048592 | tf_op jit(solution)/shard_map/all_gather | solution.py:12
  249.6 5.2 %fusion.47 = f32[64,128,128]{2,1,0:T(8,128)} fusion(bf16[64,128,128]{2,1,0:T(8,128)(2,1)} %gather_fusion.1, bf16[1,1,64,128,128]{4,3,2,1,0:T(8,128)(2,1)S(1)} %copy-done), kind=kOutput, calls=%fused_computation.97 | convolution fusion | flops 268435456 | bytes 8388608 | tf_op jit(solution)/shard_map/ntk,nks->nts/dot_general | solution.py:14
  254.8 5.5 %copy.14 = f32[64,128,128]{1,0,2:T(8,128)} copy(f32[64,128,128]{2,1,0:T(8,128)} %fusion.47) | data formatting | bytes 8388608 | tf_op jit(solution)/shard_map/ntk,nks->nts/dot_general | solution.py:14
  260.3 3.7 fusion.8
  265.4 8.0 %reduce-scatter.15.cloned.1.call-done = f32[512,128]{1,0:T(8,128)} async-done(((f32[2048,128]{1,0:T(8,128)}), f32[512,128]{1,0:T(8,128)}) %reduce-scatter.15.cloned.1.call-update) | async-done | bytes 262160 | tf_op jit(solution)/shard_map/reduce_scatter | solution.py:33
  273.4 27.6 %reduce-scatter.9.cloned.1.call-done = f32[512,128]{1,0:T(8,128)} async-done(((f32[2048,128]{1,0:T(8,128)}), f32[512,128]{1,0:T(8,128)}) %reduce-scatter.9.cloned.1.call-update) | async-done | bytes 262160 | tf_op jit(solution)/shard_map/reduce_scatter | solution.py:19
  303.5 39.5 %all-gather.17.cloned.1.call-done = bf16[4096,128]{1,0:T(8,128)(2,1)} async-done(((bf16[512,128]{1,0:T(8,128)(2,1)}), bf16[4096,128]{1,0:T(8,128)(2,1)}) %all-gather.17.cloned.1.call-update) | async-done | bytes 1048592 | tf_op jit(solution)/shard_map/all_gather | solution.py:26
  346.4 5.1 %fusion.53 = f32[64,128,128]{2,1,0:T(8,128)} fusion(bf16[64,128,128]{2,1,0:T(8,128)(2,1)} %gather_fusion.5, bf16[64,128,128]{2,1,0:T(8,128)(2,1)} %all-to-all-done), kind=kOutput, calls=%fused_computation.103 | convolution fusion | flops 268435456 | bytes 8388608 | tf_op jit(solution)/shard_map/nkt,nks->nts/dot_general | solution.py:28
  351.5 5.4 %copy.18 = f32[64,128,128]{1,0,2:T(8,128)} copy(f32[64,128,128]{2,1,0:T(8,128)} %fusion.53) | data formatting | bytes 8388608 | tf_op jit(solution)/shard_map/nkt,nks->nts/dot_general | solution.py:28
  356.9 3.7 fusion
  362.2 22.2 %all-gather.11.cloned.1.call-done = bf16[4096,128]{1,0:T(8,128)(2,1)} async-done(((bf16[512,128]{1,0:T(8,128)(2,1)}), bf16[4096,128]{1,0:T(8,128)(2,1)}) %all-gather.11.cloned.1.call-update) | async-done | bytes 1048592 | tf_op jit(solution)/shard_map/all_gather | solution.py:12
  387.9 5.2 %fusion.45 = f32[64,128,128]{2,1,0:T(8,128)} fusion(bf16[64,128,128]{2,1,0:T(8,128)(2,1)} %gather_fusion.2, bf16[1,1,64,128,128]{4,3,2,1,0:T(8,128)(2,1)S(1)} %copy-done), kind=kOutput, calls=%fused_computation.95 | convolution fusion | flops 268435456 | bytes 8388608 | tf_op jit(solution)/shard_map/ntk,nks->nts/dot_general | solution.py:14
  393.0 5.5 %copy.15 = f32[64,128,128]{1,0,2:T(8,128)} copy(f32[64,128,128]{2,1,0:T(8,128)} %fusion.45) | data formatting | bytes 8388608 | tf_op jit(solution)/shard_map/ntk,nks->nts/dot_general | solution.py:14
  398.6 3.6 fusion.6
  403.6 8.0 %reduce-scatter.17.cloned.1.call-done = f32[512,128]{1,0:T(8,128)} async-done(((f32[2048,128]{1,0:T(8,128)}), f32[512,128]{1,0:T(8,128)}) %reduce-scatter.17.cloned.1.call-update) | async-done | bytes 262160 | tf_op jit(solution)/shard_map/reduce_scatter | solution.py:33
  411.6 27.5 %reduce-scatter.11.cloned.1.call-done = f32[512,128]{1,0:T(8,128)} async-done(((f32[2048,128]{1,0:T(8,128)}), f32[512,128]{1,0:T(8,128)}) %reduce-scatter.11.cloned.1.call-update) | async-done | bytes 262160 | tf_op jit(solution)/shard_map/reduce_scatter | solution.py:19
  (67 shorter events, 36.0 us)
Async XLA Ops:
  7.2 61.9 %all-gather.7.cloned.1.call-start = ((), (), s32[]{:S(2)}) async-start(), calls=%async_computation.7 | async-start | bytes 1179648 | tf_op jit(solution)/shard_map/all_gather | solution.py:12
  9.7 8.0 %copy-start.7 = (s32[8,4,64]{2,1,0:T(4,128)S(1)}, s32[8,4,64]{2,1,0:T(4,128)}, u32[]{:S(2)}) copy-start(s32[8,4,64]{2,1,0:T(4,128)} %param.6) | copy-start | bytes 24580
  9.7 102.0 %all-to-all-start = ((bf16[64,128,128]{2,1,0:T(8,128)(2,1)}), bf16[64,128,128]{2,1,0:T(8,128)(2,1)}, u32[]{:S(2)}, u32[]{:S(2)}) async-start(bf16[64,128,128]{2,1,0:T(8,128)(2,1)} %bitcast.112), calls=%async_computation.3 | async-start | bytes 4194304 | tf_op jit(solution)/shard_map/all_to_all | solution.py:74
  16.9 91.4 %all-gather.13.cloned.1.call-start = ((), (), s32[]{:S(2)}) async-start(), calls=%async_computation.13 | async-start | bytes 1179648 | tf_op jit(solution)/shard_map/all_gather | solution.py:26
  17.6 117.9 %reduce-scatter.7.cloned.1.call-start = ((), (), s32[]{:S(2)}) async-start(), calls=%async_computation.8 | async-start | bytes 1310720 | tf_op jit(solution)/shard_map/reduce_scatter | solution.py:19
  69.0 3.6 copy-start
  88.1 74.8 %reduce-scatter.13.cloned.1.call-start = ((), (), s32[]{:S(2)}) async-start(), calls=%async_computation.14 | async-start | bytes 1310720 | tf_op jit(solution)/shard_map/reduce_scatter | solution.py:33
  127.3 77.4 %all-gather.15.cloned.1.call-start = ((), (), s32[]{:S(2)}) async-start(), calls=%async_computation.15 | async-start | bytes 1179648 | tf_op jit(solution)/shard_map/all_gather | solution.py:26
  164.8 81.4 %all-gather.9.cloned.1.call-start = ((), (), s32[]{:S(2)}) async-start(), calls=%async_computation.9 | async-start | bytes 1179648 | tf_op jit(solution)/shard_map/all_gather | solution.py:12
  165.4 108.1 %reduce-scatter.15.cloned.1.call-start = ((), (), s32[]{:S(2)}) async-start(), calls=%async_computation.16 | async-start | bytes 1310720 | tf_op jit(solution)/shard_map/reduce_scatter | solution.py:33
  223.6 77.4 %reduce-scatter.9.cloned.1.call-start = ((), (), s32[]{:S(2)}) async-start(), calls=%async_computation.10 | async-start | bytes 1310720 | tf_op jit(solution)/shard_map/reduce_scatter | solution.py:19
  265.4 77.6 %all-gather.17.cloned.1.call-start = ((), (), s32[]{:S(2)}) async-start(), calls=%async_computation.17 | async-start | bytes 1179648 | tf_op jit(solution)/shard_map/all_gather | solution.py:26
  302.8 81.6 %all-gather.11.cloned.1.call-start = ((), (), s32[]{:S(2)}) async-start(), calls=%async_computation.11 | async-start | bytes 1179648 | tf_op jit(solution)/shard_map/all_gather | solution.py:12
  303.4 108.2 %reduce-scatter.17.cloned.1.call-start = ((), (), s32[]{:S(2)}) async-start(), calls=%async_computation.18 | async-start | bytes 1310720 | tf_op jit(solution)/shard_map/reduce_scatter | solution.py:33
  361.9 77.2 %reduce-scatter.11.cloned.1.call-start = ((), (), s32[]{:S(2)}) async-start(), calls=%async_computation.12 | async-start | bytes 1310720 | tf_op jit(solution)/shard_map/reduce_scatter | solution.py:19
  402.2 36.9 %copy-start.1 = (f32[512,128]{1,0:T(8,128)S(1)}, f32[512,128]{1,0:T(8,128)}, u32[]{:S(2)}) copy-start(f32[512,128]{1,0:T(8,128)} %reduce-scatter.7.cloned.1.call-done) | copy-start | bytes 786436
  402.2 36.9 %copy-start.2 = (f32[512,128]{1,0:T(8,128)S(1)}, f32[512,128]{1,0:T(8,128)}, u32[]{:S(2)}) copy-start(f32[512,128]{1,0:T(8,128)} %reduce-scatter.13.cloned.1.call-done) | copy-start | bytes 786436
  402.2 36.9 %copy-start.3 = (f32[512,128]{1,0:T(8,128)S(1)}, f32[512,128]{1,0:T(8,128)}, u32[]{:S(2)}) copy-start(f32[512,128]{1,0:T(8,128)} %reduce-scatter.15.cloned.1.call-done) | copy-start | bytes 786436
  402.2 36.9 %copy-start.4 = (f32[512,128]{1,0:T(8,128)S(1)}, f32[512,128]{1,0:T(8,128)}, u32[]{:S(2)}) copy-start(f32[512,128]{1,0:T(8,128)} %reduce-scatter.9.cloned.1.call-done) | copy-start | bytes 786436
  402.3 36.9 %copy-start.5 = (bf16[512,128]{1,0:T(8,128)(2,1)S(1)}, bf16[512,128]{1,0:T(8,128)(2,1)}, u32[]{:S(2)}) copy-start(bf16[512,128]{1,0:T(8,128)(2,1)} %param.8) | copy-start | bytes 393220
  402.3 36.9 %copy-start.6 = (bf16[512,128]{1,0:T(8,128)(2,1)S(1)}, bf16[512,128]{1,0:T(8,128)(2,1)}, u32[]{:S(2)}) copy-start(bf16[512,128]{1,0:T(8,128)(2,1)} %param.7) | copy-start | bytes 393220
Sparse Core Ops, SparseCore 0:
  10.7 58.2 all-gather.6
  71.7 36.5 all-gather.12
  110.8 24.6 reduce-scatter.6
  138.1 24.8 reduce-scatter.12
  165.5 39.1 all-gather.14
  207.3 38.8 all-gather.8
  248.7 24.6 reduce-scatter.14
  276.1 24.8 reduce-scatter.8
  303.7 39.1 all-gather.16
  345.5 38.8 all-gather.10
  387.0 24.6 reduce-scatter.16
  414.2 24.8 reduce-scatter.10
where the time goes:
time: 450 us; the launch traced here: 448 us
  waiting for transfers between devices  303 us (67%)
  local copies, waits for them, and re-layouts  61.5 us (14%)
  matrix products  52.8 us (12%)
  between operations  14.4 us (3%)
  starting transfers between devices  8.04 us (2%)
  other arithmetic  8.04 us (2%)
    all_gather x3, waiting for transfers between devices, charge_term(): gathered = lax.all_gather(vector, 'row', axis=0, tiled=True)  98.4 us
    all_gather x3, waiting for transfers between devices, supply_term(): gathered = lax.all_gather(vector, 'row', axis=0, tiled=True)  96 us
    reduce_scatter x3, waiting for transfers between devices, supply_term(): lax.psum_scatter(partial_value.reshape(-1, scenarios), 'col', scatter_dim...  63.2 us
    reduce_scatter x3, waiting for transfers between devices, charge_term(): lax.psum_scatter(partial_value.reshape(-1, scenarios), 'col', scatter_dim...  43.5 us
    dot_general x3, local copies, waits for them, and re-layouts, supply_term(): jnp.einsum('ntk,nks->nts', own_tiles, picked, preferred_element_type=jnp....  16.5 us
    dot_general x3, local copies, waits for them, and re-layouts, charge_term(): jnp.einsum('nkt,nks->nts', moved_tiles, picked, preferred_element_type=jn...  16.3 us
    dot_general x3, matrix products, supply_term(): jnp.einsum('ntk,nks->nts', own_tiles, picked, preferred_element_type=jnp....  15.5 us
    dot_general x3, matrix products, charge_term(): jnp.einsum('nkt,nks->nts', moved_tiles, picked, preferred_element_type=jn...  15.3 us
  transfers between devices with their start and end apart: 13, of which 12 were waited for; matrix products, arithmetic and copies ran while one was open for 26% of the time, Pallas kernels for 0%

commit v1 on v0

v1 whole, which is shorter than its diff:
```python
import functools

import jax
import jax.numpy as jnp
from jax import lax
from jax.experimental import pallas as pl
from jax.experimental.pallas import tpu as pltpu
from jax.sharding import PartitionSpec as P

TERMS = 3
GROUPS = 128
LEVEL = 32000.0
MESH = pl.DeviceIdType.MESH


def pack(values, slot):
    rows = values.shape[0]
    top = jnp.max(jnp.abs(values), axis=0, keepdims=True)
    power = jnp.ceil(jnp.log2(jnp.maximum(top, 1e-30)))
    scaled = jnp.floor(values * (jnp.exp2(-power) * LEVEL) + 0.5)
    slot[pl.ds(0, rows), :] = scaled.astype(jnp.int32).astype(jnp.int16)
    slot[pl.ds(rows, 16), :] = (
        jnp.broadcast_to(power, (16, power.shape[1])).astype(jnp.int32).astype(jnp.int16)
    )


def unpack(slot, rows):
    power = slot[pl.ds(rows, 16), :].astype(jnp.int32).astype(jnp.float32)[0:1, :]
    values = slot[pl.ds(0, rows), :].astype(jnp.int32).astype(jnp.float32)
    return values * (jnp.exp2(power) * (1.0 / LEVEL))


def kernel(
    rows, columns, capacity, quarter, places, tiles, demand, value_added, gone, gone_down,
    quantity, price_out,
    stack, wide, gath_q, gath_p, here_q, here_p, spread_q, spread_p, price, total,
    send_x, send_z, send_q, got_x, got_z, got_q,
    tile_sem, out_sem, aqz_s, aqz_r, aqx_s, aqx_r, ap_s, ap_r, px_s, px_r, pz_s, pz_r, q_s, q_r,
):
    size = tiles.shape[1]
    scenarios = demand.shape[1]
    length = quarter * size
    slabs = rows // 2
    group = columns * capacity
    row, column = lax.axis_index("row"), lax.axis_index("col")
    slab, side = row // 2, row % 2
    partner = (slab * 2 + 1 - side, column)

    def slab_peer(step):
        return lax.rem(slab + step, slabs)

    def column_peer(step):
        return lax.rem(column + step, columns)

    def remote(src, dst, send, recv, device):
        return pltpu.make_async_remote_copy(
            src_ref=src, dst_ref=dst, send_sem=send, recv_sem=recv,
            device_id=device, device_id_type=MESH,
        )

    whole = pltpu.make_async_copy(tiles, stack, tile_sem.at[0])
    whole.start()

    def side_by_side(m):
        d, u = m // capacity, m % capacity
        place = pl.multiple_of(((d // columns) * capacity + u) * size, size)
        return pltpu.make_async_copy(
            tiles.at[m], wide.at[d % columns, :, pl.ds(place, size)], out_sem.at[m]
        )

    lax.fori_loop(0, rows * group, lambda m, _: (side_by_side(m).start(), 0)[1], 0)

    barrier = pltpu.get_barrier_semaphore()
    pl.semaphore_signal(barrier, inc=1, device_id=partner, device_id_type=MESH)
    for step in range(1, slabs):
        pl.semaphore_signal(
            barrier, inc=1, device_id=(slab_peer(step) * 2 + side, column), device_id_type=MESH
        )
    for step in range(1, columns):
        pl.semaphore_signal(
            barrier, inc=1, device_id=(row, column_peer(step)), device_id_type=MESH
        )

    first = (row * columns + column) * quarter
    for q in range(quarter):
        part = pl.ds(q * size, size)
        block = (first + q) % GROUPS
        keep = jnp.where(gone[...] != block, 1.0, 0.0)
        start = keep * demand[part, :].astype(jnp.float32)
        quantity[part, :] = start
        gath_q[0, row, part, :] = start.astype(jnp.bfloat16)
        keep_down = jnp.where(gone_down[...] != block, 1.0, 0.0)
        start = keep_down * value_added[part, :].astype(jnp.float32).T
        price[pl.ds(q * scenarios, scenarios), :] = start
        gath_p[0, column, pl.ds(q * scenarios, scenarios), :] = start.astype(jnp.bfloat16)

    pl.semaphore_wait(barrier, slabs + columns - 1)
    whole.wait()
    lax.fori_loop(0, rows * group, lambda m, _: (side_by_side(m).wait(), 0)[1], 0)

    def weight(ok):
        return jnp.full((16, 128), jnp.where(ok, 1.0, 0.0), jnp.float32).astype(jnp.bfloat16)

    def charge_part(t, owner):
        def fill(k, _):
            place = places[0, owner * group + k]
            at = (k // capacity) * quarter + place // quarter
            block = here_p[at // quarter, pl.ds((at % quarter) * scenarios, scenarios), :]
            block = block.reshape(scenarios // 16, 16, size)
            for q in range(quarter):
                spread_p[k, pl.ds(q * scenarios, scenarios), :] = (
                    block * weight(place % quarter == q)[None]
                ).reshape(scenarios, size)
            return 0

        lax.fori_loop(0, group, fill, 0, unroll=True)
        left = jnp.concatenate([spread_p[k] for k in range(group)], axis=1)
        right = stack[pl.ds(owner * group, group)].reshape(group * size, size)
        return jnp.dot(left, right, preferred_element_type=jnp.float32)

    def supply_part(t, owner):
        width = 4

        def chunk(j, _):
            for k in range(width * capacity):
                source = j * width + k // capacity
                place = places[0, (source * columns + owner) * capacity + k % capacity]
                block = here_q[source, pl.ds((place % quarter) * size, size), :]
                block = block.reshape(size // 16, 16, scenarios)
                for q in range(quarter):
                    spread_q[pl.ds(k * size, size), pl.ds(q * scenarios, scenarios)] = (
                        block * weight(place // quarter == q)[None]
                    ).reshape(size, scenarios)
            depth = width * capacity * size
            left = wide[owner, :, pl.ds(pl.multiple_of(j * depth, depth), depth)]
            product = jnp.dot(left, spread_q[...], preferred_element_type=jnp.float32)
            for q in range(quarter):
                part = product[:, q * scenarios : (q + 1) * scenarios]
                total[pl.ds(q * size, size), :] += part
            return 0

        total[...] = jnp.zeros_like(total)
        lax.fori_loop(0, rows // width, chunk, 0)

    def term(t, _):
        def own_over(step):
            return remote(
                gath_q.at[t, row], gath_q.at[t, row], aqz_s.at[t, step], aqz_r.at[t, slab],
                (slab_peer(step) * 2 + side, column),
            )

        def from_over(z):
            at = z * 2 + side
            return remote(
                gath_q.at[t, at], gath_q.at[t, at], aqz_s.at[t, 0], aqz_r.at[t, z], partner
            )

        def across(z):
            at = z * 2 + side
            return remote(
                gath_q.at[t, at], gath_q.at[t, at], aqx_s.at[t, z], aqx_r.at[t, z], partner
            )

        def from_across(z):
            at = z * 2 + 1 - side
            return remote(
                gath_q.at[t, at], gath_q.at[t, at], aqx_s.at[t, z], aqx_r.at[t, z], partner
            )

        def charge_to(step):
            return remote(
                gath_p.at[t, column], gath_p.at[t, column], ap_s.at[t, step],
                ap_r.at[t, column], (row, column_peer(step)),
            )

        def charge_from(c):
            return remote(
                gath_p.at[t, c], gath_p.at[t, c], ap_s.at[t, 0], ap_r.at[t, c], partner
            )

        def cost_across(z):
            return remote(
                send_x.at[z], got_x.at[t, z], px_s.at[t, z], px_r.at[t, z], partner
            )

        def cost_over(step):
            return remote(
                send_z.at[step], got_z.at[t, slab], pz_s.at[t, step], pz_r.at[t, slab],
                (slab_peer(step) * 2 + side, column),
            )

        def cost_from(z):
            return remote(
                send_z.at[0], got_z.at[t, z], pz_s.at[t, 0], pz_r.at[t, z], partner
            )

        def image_to(step):
            return remote(
                send_q.at[step], got_q.at[t, column], q_s.at[t, step], q_r.at[t, column],
                (row, column_peer(step)),
            )

        def image_from(c):
            return remote(
                send_q.at[0], got_q.at[t, c], q_s.at[t, 0], q_r.at[t, c], partner
            )

        def each(low, high, body):
            lax.fori_loop(low, high, lambda i, _: (body(i), 0)[1], 0)

        each(1, columns, lambda s: charge_to(s).start())
        each(1, slabs, lambda s: own_over(s).start())
        across(slab).start()

        each(1, columns, lambda s: charge_from(column_peer(s)).wait_recv())
        here_p[...] = gath_p[t]

        def give_across(s):
            z = slab_peer(s)
            pack(charge_part(t, z * 2 + 1 - side), send_x.at[z])
            cost_across(z).start()

        each(1, slabs + 1, give_across)

        def forward(s):
            z = slab_peer(s)
            from_over(z).wait_recv()
            across(z).start()

        each(1, slabs, forward)

        def give_over(s):
            z = slab_peer(s)
            mine = charge_part(t, z * 2 + side)
            cost_across(z).wait_recv()
            pack(mine + unpack(got_x.at[t, z], length), send_z.at[s])
            cost_over(s).start()

        each(1, slabs, give_over)

        each(0, slabs, lambda z: from_across(z).wait_recv())

        def bring(i):
            here_q[i] = gath_q[t, i]

        each(0, rows, bring)

        def give_image(s):
            supply_part(t, column_peer(s))
            pack(total[...], send_q.at[s])
            image_to(s).start()

        each(1, columns, give_image)
        supply_part(t, column)
        image = total[...]
        for s in range(1, columns):
            c = column_peer(s)
            image_from(c).wait_recv()
            image += unpack(got_q.at[t, c], length)
        for q in range(quarter):
            part = pl.ds(q * size, size)
            keep = jnp.where(gone[...] != (first + q) % GROUPS, 1.0, 0.0)
            masked = keep * image[q * size : (q + 1) * size]
            quantity[part, :] += masked
            gath_q[lax.rem(t + 1, TERMS), row, part, :] = masked.astype(jnp.bfloat16)

        mine = charge_part(t, row)
        cost_across(slab).wait_recv()
        total[...] = mine + unpack(got_x.at[t, slab], length)

        def take_over(s):
            z = slab_peer(s)
            cost_from(z).wait_recv()
            total[...] += unpack(got_z.at[t, z], length)

        each(1, slabs, take_over)
        for q in range(quarter):
            part = pl.ds(q * scenarios, scenarios)
            keep_down = jnp.where(gone_down[...] != (first + q) % GROUPS, 1.0, 0.0)
            masked = keep_down * total[part, :]
            price[part, :] += masked
            gath_p[lax.rem(t + 1, TERMS), column, part, :] = masked.astype(jnp.bfloat16)

        each(1, columns, lambda s: charge_to(s).wait_send())
        each(1, slabs, lambda s: own_over(s).wait_send())
        each(0, slabs, lambda z: across(z).wait_send())
        each(0, slabs, lambda z: cost_across(z).wait_send())
        each(1, slabs, lambda s: cost_over(s).wait_send())
        each(1, columns, lambda s: image_to(s).wait_send())
        return 0

    lax.fori_loop(0, TERMS, term, 0)
    for q in range(quarter):
        price_out[pl.ds(q * size, size), :] = price[pl.ds(q * scenarios, scenarios), :].T


def shards(tiles, positions, demand, value_added, extracted):
    rows, columns = lax.axis_size("row"), lax.axis_size("col")
    slots, size = tiles.shape[2], tiles.shape[-1]
    length, scenarios = demand.shape
    quarter = length // size
    capacity = slots // (rows * columns)
    slabs = rows // 2
    places = lax.dynamic_slice(
        positions, (lax.axis_index("row"), lax.axis_index("col"), 0), (1, 1, slots)
    ).reshape(1, slots)
    dma = pltpu.SemaphoreType.DMA
    vmem = pl.BlockSpec(memory_space=pltpu.VMEM)
    bf16, f32, i16 = jnp.bfloat16, jnp.float32, jnp.int16
    packed = (length + 16, scenarios)
    return pl.pallas_call(
        functools.partial(kernel, rows, columns, capacity, quarter),
        out_shape=(
            jax.ShapeDtypeStruct((length, scenarios), f32),
            jax.ShapeDtypeStruct((length, scenarios), f32),
        ),
        in_specs=[
            pl.BlockSpec(memory_space=pltpu.SMEM),
            pl.BlockSpec(memory_space=pl.ANY),
            vmem, vmem, vmem, vmem,
        ],
        out_specs=(vmem, vmem),
        scratch_shapes=[
            pltpu.VMEM((slots, size, size), bf16),
            pltpu.VMEM((columns, size, rows * capacity * size), bf16),
            pltpu.VMEM((TERMS, rows, length, scenarios), bf16),
            pltpu.VMEM((TERMS, columns, quarter * scenarios, size), bf16),
            pltpu.VMEM((rows, length, scenarios), bf16),
            pltpu.VMEM((columns, quarter * scenarios, size), bf16),
            pltpu.VMEM((4 * capacity * size, quarter * scenarios), bf16),
            pltpu.VMEM((columns * capacity, quarter * scenarios, size), bf16),
            pltpu.VMEM((quarter * scenarios, size), f32),
            pltpu.VMEM((length, scenarios), f32),
            pltpu.VMEM((slabs,) + packed, i16),
            pltpu.VMEM((slabs,) + packed, i16),
            pltpu.VMEM((columns,) + packed, i16),
            pltpu.VMEM((TERMS, slabs) + packed, i16),
            pltpu.VMEM((TERMS, slabs) + packed, i16),
            pltpu.VMEM((TERMS, columns) + packed, i16),
            dma((1,)), dma((slots,)),
            dma((TERMS, slabs)), dma((TERMS, slabs)), dma((TERMS, slabs)), dma((TERMS, slabs)),
            dma((TERMS, columns)), dma((TERMS, columns)),
            dma((TERMS, slabs)), dma((TERMS, slabs)), dma((TERMS, slabs)), dma((TERMS, slabs)),
            dma((TERMS, columns)), dma((TERMS, columns)),
        ],
        compiler_params=pltpu.CompilerParams(
            collective_id=0, has_side_effects=True, vmem_limit_bytes=60 * 2**20
        ),
        name="series",
    )(
        places,
        tiles.reshape(slots, size, size),
        demand,
        value_added,
        extracted.reshape(1, scenarios),
        extracted.reshape(scenarios, 1),
    )


def solution(mesh):
    placed = (
        P("row", "col", None, None, None),
        P(),
        P(("row", "col"), None),
        P(("row", "col"), None),
        P(),
    )
    return jax.shard_map(
        shards,
        mesh=mesh,
        in_specs=placed,
        out_specs=(P(("row", "col"), None), P(("row", "col"), None)),
        check_vma=False,
    )
```

time: 450 us -> 130 us (0.29)
  waiting for transfers between devices: 303 us -> 0 us
  Pallas kernels: 0 us -> 123 us
  local copies, waits for them, and re-layouts: 61.5 us -> 5.95 us
  matrix products: 52.8 us -> 0 us
  between operations: 14.4 us -> 0.65 us
  other arithmetic: 8.04 us -> 0 us
  starting transfers between devices: 8.04 us -> 0 us
    all_gather x6 -> x0, waiting for transfers between devices: 194 us -> none  [the longest x3 98.4 us: charge_term(): gathered = lax.all_gather(vector, 'row', axis=0, tiled=True)]
    pallas_call x0 -> x1, Pallas kernels: none -> 123 us  [shards(): pl.pallas_call(functools.partial(kernel, rows, columns, capacity, quarter...]
    reduce_scatter x6 -> x0, waiting for transfers between devices: 107 us -> none  [the longest x3 63.2 us: supply_term(): lax.psum_scatter(partial_value.reshape(-1, scenarios), 'col', scatter_dim...]
    dot_general x12 -> x0, matrix products: 52.8 us -> none  [the longest x3 15.5 us: supply_term(): jnp.einsum('ntk,nks->nts', own_tiles, picked, preferred_element_type=jnp....]
    dot_general x12 -> x0, local copies, waits for them, and re-layouts: 40.7 us -> none  [the longest x3 16.5 us: supply_term(): jnp.einsum('ntk,nks->nts', own_tiles, picked, preferred_element_type=jnp....]
    gather x6 -> x0, local copies, waits for them, and re-layouts: 20.5 us -> none  [the longest x3 10.3 us: supply_term(): picked = gathered.reshape(-1, tile_size, scenarios)[local_columns]]
    all_to_all x1 -> x0, starting transfers between devices: 7.16 us -> none  [shards(): lax.all_to_all(own_tiles, ('row', 'col'), split_axis=0, concat_axis=0, ti...]
    convert_element_type x4 -> x0, other arithmetic: 5.99 us -> none  [the longest x2 3.54 us: shards(): charge = masked.astype(jnp.bfloat16)]
  transfers between devices with their start and end apart: 13 -> 0, of which waited for: 12 -> 0; matrix products, arithmetic and copies ran while one was open for 26% -> 0% of each run, Pallas kernels for 0% -> 0%
where the time goes in v1:
time: 130 us
  Pallas kernels  123 us (95%)
  local copies, waits for them, and re-layouts  5.95 us (5%)
    pallas_call x1, Pallas kernels, shards(): pl.pallas_call(functools.partial(kernel, rows, columns, capacity, quarter...  123 us
    unnamed x4, local copies, waits for them, and re-layouts  4.05 us

profile of v1, /device:TPU:1, one launch (start us, length us, event | category | flops | bytes accessed | tf_op | source)
XLA Modules:
  0.0 129.7 jit_solution(17789851986678432255)
XLA Ops:
  0.6 0.0 copy-start
  0.6 0.7 copy-done
  1.4 0.5 dynamic-slice_bitcast_fusion.places
  1.9 1.4 %copy.7.gone_down = s32[128,1]{1,0:T(8,128)} copy(s32[128,1]{0,1:T(1,128)} %bitcast.6) | data formatting | bytes 1024 | tf_op jit(solution)/shard_map/reshape | solution.py:356
  3.3 123.1 %series.1 = (f32[512,128]{1,0:T(8,128)}, f32[512,128]{1,0:T(8,128)}) custom-call(s32[1,64]{1,0:T(1,128)} %dynamic-slice_bitcast_fusion.places, bf16[64,128,128]{2,1,0:T(8,128)(2,1)} %bitcast.5, bf16[512,128]{1,0:T(8,128)(2,1)} %demand.1, bf16[512,128]{1,0:T(8,128)(2,1)} %value_added.1, s32[1,128]{1,0:T(1,128)} %bitcast.7, s32[128,1]{1,0:T(8,128)} %copy.7.gone_down), custom_call_target="tpu_custom_call" | custom-call | tf_op jit(solution)/shard_map/series/pallas_call | solution.py:311
  126.3 1.7 %copy.10 = f32[512,128]{1,0:T(8,128)} copy(f32[512,128]{1,0:T(8,128)} %get-tuple-element.4) | data formatting | bytes 524288
  128.0 1.7 %copy.11 = f32[512,128]{1,0:T(8,128)} copy(f32[512,128]{1,0:T(8,128)} %get-tuple-element.5) | data formatting | bytes 524288
Async XLA Ops:
  0.6 0.7 copy-start

commit v2 on v1

v2 whole, which is shorter than its diff:
```python
import functools

import jax
import jax.numpy as jnp
from jax import lax
from jax.experimental import pallas as pl
from jax.experimental.pallas import tpu as pltpu
from jax.sharding import PartitionSpec as P

TERMS = 3
GROUPS = 128
LEVEL = 32000.0
MESH = pl.DeviceIdType.MESH


def pack(values, slot):
    rows = values.shape[0]
    top = jnp.max(jnp.abs(values), axis=0, keepdims=True)
    power = jnp.ceil(jnp.log2(jnp.maximum(top, 1e-30)))
    scaled = jnp.floor(values * (jnp.exp2(-power) * LEVEL) + 0.5)
    slot[pl.ds(0, rows), :] = scaled.astype(jnp.int32).astype(jnp.int16)
    slot[pl.ds(rows, 16), :] = (
        jnp.broadcast_to(power, (16, power.shape[1])).astype(jnp.int32).astype(jnp.int16)
    )


def unpack(slot, rows):
    power = slot[pl.ds(rows, 16), :].astype(jnp.int32).astype(jnp.float32)[0:1, :]
    values = slot[pl.ds(0, rows), :].astype(jnp.int32).astype(jnp.float32)
    return values * (jnp.exp2(power) * (1.0 / LEVEL))


def kernel(
    rows, columns, capacity, quarter, places, tiles, demand, value_added, gone,
    quantity, price_out,
    stack, wide, gath_q, gath_p, here_q, here_p, spread_q, spread_p, price, total, keep_down,
    send_x, send_z, send_q, got_x, got_z, got_q,
    tile_sem, out_sem, up_s, down_s, over_r, aqx_s, aqx_r, ap_s, ap_r, px_s, px_r, pz_s, pz_r, q_s, q_r,
):
    size = tiles.shape[1]
    scenarios = demand.shape[1]
    length = quarter * size
    slabs = rows // 2
    group = columns * capacity
    row, column = lax.axis_index("row"), lax.axis_index("col")
    slab, side = row // 2, row % 2
    partner = (slab * 2 + 1 - side, column)

    last = slabs - 1

    def column_peer(step):
        return lax.rem(column + step, columns)

    def remote(src, dst, send, recv, device):
        return pltpu.make_async_remote_copy(
            src_ref=src, dst_ref=dst, send_sem=send, recv_sem=recv,
            device_id=device, device_id_type=MESH,
        )

    whole = pltpu.make_async_copy(tiles, stack, tile_sem.at[0])
    whole.start()

    def side_by_side(m):
        d, u = m // capacity, m % capacity
        place = pl.multiple_of(((d // columns) * capacity + u) * size, size)
        return pltpu.make_async_copy(
            tiles.at[m], wide.at[d % columns, :, pl.ds(place, size)], out_sem.at[m]
        )

    lax.fori_loop(0, rows * group, lambda m, _: (side_by_side(m).start(), 0)[1], 0)

    barrier = pltpu.get_barrier_semaphore()

    def greet(device):
        pl.semaphore_signal(barrier, inc=1, device_id=device, device_id_type=MESH)

    greet(partner)
    pl.when(slab > 0)(lambda: greet((row - 2, column)))
    pl.when(slab < last)(lambda: greet((row + 2, column)))
    for step in range(1, columns):
        greet((row, column_peer(step)))

    first = (row * columns + column) * quarter
    for q in range(quarter):
        part = pl.ds(q * size, size)
        block = (first + q) % GROUPS
        keep = jnp.where(gone[...] != block, 1.0, 0.0)
        start = keep * demand[part, :].astype(jnp.float32)
        quantity[part, :] = start
        gath_q[0, row, part, :] = start.astype(jnp.bfloat16)
        part = pl.ds(q * scenarios, scenarios)
        down = jnp.broadcast_to(keep, (size, scenarios)).T
        keep_down[part, :] = down
        start = down * value_added[pl.ds(q * size, size), :].astype(jnp.float32).T
        price[part, :] = start
        gath_p[0, column, part, :] = start.astype(jnp.bfloat16)

    def move_up(t, z):
        at = gath_q.at[t, z * 2 + side]
        return remote(at, at, up_s.at[t, z], over_r.at[t, z], (row + 2, column))

    def move_down(t, z):
        at = gath_q.at[t, z * 2 + side]
        return remote(at, at, down_s.at[t, z], over_r.at[t, z], (row - 2, column))

    def move_across(t, z):
        at = gath_q.at[t, z * 2 + side]
        return remote(at, at, aqx_s.at[t, z], aqx_r.at[t, z], partner)

    def move_from_across(t, z):
        at = gath_q.at[t, z * 2 + 1 - side]
        return remote(at, at, aqx_s.at[t, z], aqx_r.at[t, z], partner)

    def charge_to(t, step):
        at = gath_p.at[t, column]
        return remote(at, at, ap_s.at[t, step], ap_r.at[t, column], (row, column_peer(step)))

    def charge_from(t, c):
        at = gath_p.at[t, c]
        return remote(at, at, ap_s.at[t, 0], ap_r.at[t, c], partner)

    def cost_across(t, z):
        return remote(send_x.at[z], got_x.at[t, z], px_s.at[t, z], px_r.at[t, z], partner)

    def cost_up(t, z):
        return remote(
            send_z.at[z], got_z.at[t, z], pz_s.at[t, z], pz_r.at[t, z], (row + 2, column)
        )

    def cost_down(t, z):
        slot = jnp.where(z == slab - 1, slabs, z)
        return remote(
            send_z.at[z], got_z.at[t, slot], pz_s.at[t, z], pz_r.at[t, slot], (row - 2, column)
        )

    def cost_in(t, slot):
        return remote(send_z.at[0], got_z.at[t, slot], pz_s.at[t, 0], pz_r.at[t, slot], partner)

    def image_to(t, step):
        return remote(
            send_q.at[step], got_q.at[t, column], q_s.at[t, step], q_r.at[t, column],
            (row, column_peer(step)),
        )

    def image_from(t, c):
        return remote(send_q.at[0], got_q.at[t, c], q_s.at[t, 0], q_r.at[t, c], partner)

    def each(low, high, body):
        lax.fori_loop(low, high, lambda i, _: (body(i), 0)[1], 0)

    def send_charge(t):
        each(1, columns, lambda s: charge_to(t, s).start())

    def send_move(t):
        pl.when(slab < last)(lambda: move_up(t, slab).start())
        pl.when(slab > 0)(lambda: move_down(t, slab).start())
        move_across(t, slab).start()

    ends = jnp.where(slab > 0, 1, 0) + jnp.where(slab < last, 1, 0)
    pl.semaphore_wait(barrier, columns + ends)
    send_charge(0)
    send_move(0)
    whole.wait()
    lax.fori_loop(0, rows * group, lambda m, _: (side_by_side(m).wait(), 0)[1], 0)

    def weight(ok):
        return jnp.full((16, 128), jnp.where(ok, 1.0, 0.0), jnp.float32).astype(jnp.bfloat16)

    def charge_part(owner):
        def fill(k, _):
            place = places[row, column, owner * group + k]
            at = (k // capacity) * quarter + place // quarter
            block = here_p[at // quarter, pl.ds((at % quarter) * scenarios, scenarios), :]
            block = block.reshape(scenarios // 16, 16, size)
            for q in range(quarter):
                spread_p[k, pl.ds(q * scenarios, scenarios), :] = (
                    block * weight(place % quarter == q)[None]
                ).reshape(scenarios, size)
            return 0

        lax.fori_loop(0, group, fill, 0, unroll=True)
        left = jnp.concatenate([spread_p[k] for k in range(group)], axis=1)
        right = stack[pl.ds(owner * group, group)].reshape(group * size, size)
        return jnp.dot(left, right, preferred_element_type=jnp.float32)

    def supply_part(owner):
        width = 4

        def chunk(j, _):
            for k in range(width * capacity):
                source = j * width + k // capacity
                place = places[row, column, (source * columns + owner) * capacity + k % capacity]
                block = here_q[source, pl.ds((place % quarter) * size, size), :]
                block = block.reshape(size // 16, 16, scenarios)
                for q in range(quarter):
                    spread_q[pl.ds(k * size, size), pl.ds(q * scenarios, scenarios)] = (
                        block * weight(place // quarter == q)[None]
                    ).reshape(size, scenarios)
            depth = width * capacity * size
            left = wide[owner, :, pl.ds(pl.multiple_of(j * depth, depth), depth)]
            product = jnp.dot(left, spread_q[...], preferred_element_type=jnp.float32)
            for q in range(quarter):
                part = product[:, q * scenarios : (q + 1) * scenarios]
                total[pl.ds(q * size, size), :] += part
            return 0

        total[...] = jnp.zeros_like(total)
        lax.fori_loop(0, rows // width, chunk, 0)

    def owner_slab(j):
        falling = jnp.where(last - j > slab, last - j, last - j - 1)
        rising = jnp.where(j < slab, j, j + 1)
        other = jnp.where(slab < slabs // 2, falling, rising)
        return jnp.where(j == last, slab, other)

    def term(t, _):
        def pass_on(s):
            @pl.when(slab >= s)
            def _():
                z = slab - s
                move_down(t, z).wait_recv()
                pl.when(slab < last)(lambda: move_up(t, z).start())
                move_across(t, z).start()

            @pl.when(slab + s <= last)
            def _():
                z = slab + s
                move_down(t, z).wait_recv()
                pl.when(slab > 0)(lambda: move_down(t, z).start())
                move_across(t, z).start()

        def give_across(j):
            z = owner_slab(j)
            pack(charge_part(z * 2 + 1 - side), send_x.at[z])
            cost_across(t, z).start()

        def give_on(j):
            z = owner_slab(j)
            total[...] = charge_part(z * 2 + side)
            cost_across(t, z).wait_recv()
            total[...] += unpack(got_x.at[t, z], length)

            @pl.when(jnp.where(z > slab, slab > 0, slab < last))
            def _():
                cost_in(t, z).wait_recv()
                total[...] += unpack(got_z.at[t, z], length)

            pack(total[...], send_z.at[z])
            pl.when(z > slab)(lambda: cost_up(t, z).start())
            pl.when(z < slab)(lambda: cost_down(t, z).start())

        def give_image(s):
            supply_part(column_peer(s))
            pack(total[...], send_q.at[s])
            image_to(t, s).start()

        pass_on(1)
        each(1, columns, lambda s: charge_from(t, column_peer(s)).wait_recv())
        here_p[...] = gath_p[t]

        def both(j):
            give_across(j)
            pass_on(j + 2)

        each(0, slabs - 2, both)
        each(slabs - 2, slabs, give_across)
        give_on(0)
        each(0, slabs, lambda z: move_from_across(t, z).wait_recv())

        def bring(i):
            here_q[i] = gath_q[t, i]

        each(0, rows, bring)
        each(1, columns, give_image)
        each(1, last, give_on)

        supply_part(column)
        image = total[...]
        for s in range(1, columns):
            c = column_peer(s)
            image_from(t, c).wait_recv()
            image += unpack(got_q.at[t, c], length)
        for q in range(quarter):
            part = pl.ds(q * size, size)
            keep = jnp.where(gone[...] != (first + q) % GROUPS, 1.0, 0.0)
            masked = keep * image[q * size : (q + 1) * size]
            quantity[part, :] += masked
            gath_q[lax.rem(t + 1, TERMS), row, part, :] = masked.astype(jnp.bfloat16)
        pl.when(t + 1 < TERMS)(lambda: send_move(t + 1))

        total[...] = charge_part(row)
        cost_across(t, slab).wait_recv()
        total[...] += unpack(got_x.at[t, slab], length)

        @pl.when(slab > 0)
        def _():
            cost_in(t, slab).wait_recv()
            total[...] += unpack(got_z.at[t, slab], length)

        @pl.when(slab < last)
        def _():
            cost_in(t, slabs).wait_recv()
            total[...] += unpack(got_z.at[t, slabs], length)

        masked = keep_down[...] * total[...]
        price[...] += masked
        gath_p[lax.rem(t + 1, TERMS), column] = masked.astype(jnp.bfloat16)
        pl.when(t + 1 < TERMS)(lambda: send_charge(t + 1))

        each(1, columns, lambda s: charge_to(t, s).wait_send())
        each(1, columns, lambda s: image_to(t, s).wait_send())
        each(0, slabs, lambda z: move_across(t, z).wait_send())
        each(0, slabs, lambda z: cost_across(t, z).wait_send())
        pl.when(slab < last)(lambda: each(0, slab + 1, lambda z: move_up(t, z).wait_send()))
        pl.when(slab > 0)(lambda: each(slab, slabs, lambda z: move_down(t, z).wait_send()))
        each(0, last, lambda j: cost_up(t, owner_slab(j)).wait_send())
        return 0

    lax.fori_loop(0, TERMS, term, 0)
    for q in range(quarter):
        price_out[pl.ds(q * size, size), :] = price[pl.ds(q * scenarios, scenarios), :].T


def shards(tiles, positions, demand, value_added, extracted):
    rows, columns = lax.axis_size("row"), lax.axis_size("col")
    slots, size = tiles.shape[2], tiles.shape[-1]
    length, scenarios = demand.shape
    quarter = length // size
    capacity = slots // (rows * columns)
    slabs = rows // 2
    dma = pltpu.SemaphoreType.DMA
    vmem = pl.BlockSpec(memory_space=pltpu.VMEM)
    bf16, f32, i16 = jnp.bfloat16, jnp.float32, jnp.int16
    packed = (length + 16, scenarios)
    return pl.pallas_call(
        functools.partial(kernel, rows, columns, capacity, quarter),
        out_shape=(
            jax.ShapeDtypeStruct((length, scenarios), f32),
            jax.ShapeDtypeStruct((length, scenarios), f32),
        ),
        in_specs=[
            pl.BlockSpec(memory_space=pltpu.SMEM),
            pl.BlockSpec(memory_space=pl.ANY),
            vmem, vmem, vmem,
        ],
        out_specs=(vmem, vmem),
        scratch_shapes=[
            pltpu.VMEM((slots, size, size), bf16),
            pltpu.VMEM((columns, size, rows * capacity * size), bf16),
            pltpu.VMEM((TERMS, rows, length, scenarios), bf16),
            pltpu.VMEM((TERMS, columns, quarter * scenarios, size), bf16),
            pltpu.VMEM((rows, length, scenarios), bf16),
            pltpu.VMEM((columns, quarter * scenarios, size), bf16),
            pltpu.VMEM((4 * capacity * size, quarter * scenarios), bf16),
            pltpu.VMEM((columns * capacity, quarter * scenarios, size), bf16),
            pltpu.VMEM((quarter * scenarios, size), f32),
            pltpu.VMEM((length, scenarios), f32),
            pltpu.VMEM((quarter * scenarios, size), f32),
            pltpu.VMEM((slabs,) + packed, i16),
            pltpu.VMEM((slabs,) + packed, i16),
            pltpu.VMEM((columns,) + packed, i16),
            pltpu.VMEM((TERMS, slabs) + packed, i16),
            pltpu.VMEM((TERMS, slabs + 1) + packed, i16),
            pltpu.VMEM((TERMS, columns) + packed, i16),
            dma((1,)), dma((slots,)),
            dma((TERMS, slabs)), dma((TERMS, slabs)), dma((TERMS, slabs)),
            dma((TERMS, slabs)), dma((TERMS, slabs)),
            dma((TERMS, columns)), dma((TERMS, columns)),
            dma((TERMS, slabs)), dma((TERMS, slabs)),
            dma((TERMS, slabs)), dma((TERMS, slabs + 1)),
            dma((TERMS, columns)), dma((TERMS, columns)),
        ],
        compiler_params=pltpu.CompilerParams(
            collective_id=0, has_side_effects=True, vmem_limit_bytes=61 * 2**20
        ),
        name="series",
    )(
        positions,
        tiles.reshape(slots, size, size),
        demand,
        value_added,
        extracted.reshape(1, scenarios),
    )


def solution(mesh):
    placed = (
        P("row", "col", None, None, None),
        P(),
        P(("row", "col"), None),
        P(("row", "col"), None),
        P(),
    )
    return jax.shard_map(
        shards,
        mesh=mesh,
        in_specs=placed,
        out_specs=(P(("row", "col"), None), P(("row", "col"), None)),
        check_vma=False,
    )
```

time: 130 us -> 113 us (0.87)
  Pallas kernels: 123 us -> 109 us
  local copies, waits for them, and re-layouts: 5.95 us -> 3.34 us
    pallas_call x1, Pallas kernels: 123 us -> 109 us  [shards(): pl.pallas_call(functools.partial(kernel, rows, columns, capacity, quarter...]
    reshape x2 -> x0, local copies, waits for them, and re-layouts: 1.9 us -> none  [the longest x1 1.39 us: shards(): extracted.reshape(scenarios, 1)]
    unnamed x4 -> x2, local copies, waits for them, and re-layouts: 4.05 us -> 3.34 us
where the time goes in v2:
time: 113 us
  Pallas kernels  109 us (96%)
  local copies, waits for them, and re-layouts  3.34 us (3%)
    pallas_call x1, Pallas kernels, shards(): pl.pallas_call(functools.partial(kernel, rows, columns, capacity, quarter...  109 us
    unnamed x2, local copies, waits for them, and re-layouts  3.34 us

profile of v2, /device:TPU:1, one launch (start us, length us, event | category | flops | bytes accessed | tf_op | source)
XLA Modules:
  0.0 112.8 jit_solution(9914751308747527119)
XLA Ops:
  0.6 108.8 %series.1 = (f32[512,128]{1,0:T(8,128)}, f32[512,128]{1,0:T(8,128)}) custom-call(s32[8,4,64]{2,1,0:T(4,128)} %places.1, bf16[64,128,128]{2,1,0:T(8,128)(2,1)} %bitcast.2, bf16[512,128]{1,0:T(8,128)(2,1)} %demand.1, bf16[512,128]{1,0:T(8,128)(2,1)} %value_added.1, s32[1,128]{1,0:T(1,128)} %bitcast.3), custom_call_target="tpu_custom_call" | custom-call | tf_op jit(solution)/shard_map/series/pallas_call | solution.py:335
  109.4 1.7 %copy.9 = f32[512,128]{1,0:T(8,128)} copy(f32[512,128]{1,0:T(8,128)} %get-tuple-element.4) | data formatting | bytes 524288
  111.1 1.7 %copy.10 = f32[512,128]{1,0:T(8,128)} copy(f32[512,128]{1,0:T(8,128)} %get-tuple-element.5) | data formatting | bytes 524288

commit v3 on v2

--- a/solution.py
+++ b/solution.py
@@ -264,7 +264,7 @@
 
         each(0, slabs - 2, both)
         each(slabs - 2, slabs, give_across)
-        give_on(0)
+        each(0, last, give_on)
         each(0, slabs, lambda z: move_from_across(t, z).wait_recv())
 
         def bring(i):
@@ -272,7 +272,6 @@
 
         each(0, rows, bring)
         each(1, columns, give_image)
-        each(1, last, give_on)
 
         supply_part(column)
         image = total[...]

time: 113 us -> 110 us (0.973)
  Pallas kernels: 109 us -> 106 us
    pallas_call x1, Pallas kernels: 109 us -> 106 us  [shards(): pl.pallas_call(functools.partial(kernel, rows, columns, capacity, quarter...]
where the time goes in v3:
time: 110 us
  Pallas kernels  106 us (96%)
  local copies, waits for them, and re-layouts  3.34 us (3%)
    pallas_call x1, Pallas kernels, shards(): pl.pallas_call(functools.partial(kernel, rows, columns, capacity, quarter...  106 us
    unnamed x2, local copies, waits for them, and re-layouts  3.34 us

profile of v3, /device:TPU:1, one launch (start us, length us, event | category | flops | bytes accessed | tf_op | source)
XLA Modules:
  0.0 110.1 jit_solution(3226752167903370026)
XLA Ops:
  0.6 106.1 %series.1 = (f32[512,128]{1,0:T(8,128)}, f32[512,128]{1,0:T(8,128)}) custom-call(s32[8,4,64]{2,1,0:T(4,128)} %places.1, bf16[64,128,128]{2,1,0:T(8,128)(2,1)} %bitcast.2, bf16[512,128]{1,0:T(8,128)(2,1)} %demand.1, bf16[512,128]{1,0:T(8,128)(2,1)} %value_added.1, s32[1,128]{1,0:T(1,128)} %bitcast.3), custom_call_target="tpu_custom_call" | custom-call | tf_op jit(solution)/shard_map/series/pallas_call | solution.py:334
  106.7 1.7 %copy.9 = f32[512,128]{1,0:T(8,128)} copy(f32[512,128]{1,0:T(8,128)} %get-tuple-element.4) | data formatting | bytes 524288
  108.4 1.7 %copy.10 = f32[512,128]{1,0:T(8,128)} copy(f32[512,128]{1,0:T(8,128)} %get-tuple-element.5) | data formatting | bytes 524288
